TPU v7x, 32 devices: a whole 2x2x4 slice. The times are simulated.
32 devices in a mesh: groups: 2 (over y), seq: 4 (over z), dp: 2 (over x), head: 2 (over core).
Axes of the slice: x: 2, y: 2, z: 4, core: 2. Of those that a mesh axis runs over, the one named last changes fastest.
Arguments:
- latents: bfloat16 [4, 8, 512, 1024], P(('groups', 'dp'), None, 'seq', 'head'), parts along dimension 0, may hold values from -6 to 6
- log_decay: bfloat16 [4, 8, 512, 8], P(('groups', 'dp'), None, 'seq', 'head'), parts along dimension 0, may hold values from -1 to 0, as said below
- seg_lengths: int32 [4, 4], P(('groups', 'dp')), parts along dimension 0, may hold values from 1 to 2048, 4096 in all within a row
- qkv_weight: bfloat16 [1024, 3, 1024], P('seq', None, 'head'), may hold values from -0.1875 to 0.1875
- out_weight: bfloat16 [1024, 1024], P('seq', 'head'), may hold values from -0.1875 to 0.1875
- cotangent: bfloat16 [4, 8, 512, 1024], P(('groups', 'dp'), 'seq', None, 'head'), parts along dimension 0, may hold values from -6 to 6
Outputs:
- layer_out: bfloat16 [4, 8, 512, 1024], P(('groups', 'dp'), 'seq', None, 'head'), parts along dimension 0
- output_weight_gradient: float32 [2048, 1024], P(('groups', 'seq'), 'head'), parts along dimension 0
There are 2 independent parts, one for each index of `groups`. A program takes and returns all parts, laid end to end along the dimension named above; an argument that names none is the same for every part. Nothing has to cross between parts.
Inputs may be any that keep to these rules, and one draw needn't show every extreme that they name: `log_decay`: never positive. `seg_lengths`: each row sums to 4096; a segment's state is reset at its first token.
All inputs are finite; a program needn't handle non-finite values.
Results may differ from a plain program's by a relative error of at most 0.0073.
Values may be sent and summed in bfloat16 or wider, within the bound.
A program may use at most 64 MiB of HBM per device.

v0:
```python
from functools import partial

import jax
import jax.numpy as jnp
from jax import lax
from jax.sharding import PartitionSpec as P


def shifted(value, axis, steps):
    count = lax.axis_size(axis)
    initial, last = (max(0, -steps), min(count, count - steps))
    return lax.ppermute(value, axis, [(source, source + steps) for source in range(initial, last)])


def block_step(carry_state, queries, key_rows, values_in, log_rates, segment, previous):
    head_scale = queries.shape[-1] ** (-0.5)
    cumulative = jnp.cumsum(log_rates, axis=-1)
    size_here = log_rates.shape[-1]
    order_idx = jnp.arange(size_here)
    allowed = (order_idx[:, None] >= order_idx[None, :]) & (segment[:, None] == segment[None, :])
    spread = cumulative[:, :, None] - cumulative[:, None, :]
    weight = jnp.where(allowed[None], jnp.exp(jnp.where(allowed[None], spread, 0.0)), 0.0)
    scores = jnp.einsum("htd,hsd->hts", queries, key_rows, preferred_element_type=jnp.float32)
    mixing = (scores * head_scale * weight).astype(jnp.bfloat16)
    inner_sum = jnp.einsum("hts,hsd->htd", mixing, values_in, preferred_element_type=jnp.float32)
    kept_mask = (segment == previous).astype(jnp.float32)
    carried = jnp.einsum(
        "htd,hde->hte", queries.astype(jnp.float32), carry_state, precision=lax.Precision.HIGHEST
    )
    result = (
        inner_sum
        + kept_mask[None, :, None] * jnp.exp(cumulative)[:, :, None] * carried * head_scale
    )
    last_seg = segment[-1]
    tail_decay = (
        jnp.exp(cumulative[:, -1:] - cumulative)
        * (segment == last_seg).astype(jnp.float32)[None, :]
    )
    decayed = (key_rows.astype(jnp.float32) * tail_decay[:, :, None]).astype(jnp.bfloat16)
    fresh = jnp.einsum("hsd,hse->hde", decayed, values_in, preferred_element_type=jnp.float32)
    through = jnp.exp(cumulative[:, -1]) * (last_seg == previous).astype(jnp.float32)
    return (through[:, None, None] * carry_state + fresh, result)


def to_blocks(array, count):
    moved = array.reshape((array.shape[0], count, array.shape[1] // count) + array.shape[2:])
    return jnp.moveaxis(moved, 1, 0)


def local_pass(queries, key_rows, values_in, log_rates, segment, before, block_size):
    heads_here, length, head_dim = queries.shape
    count = length // block_size
    seg_blocks = segment.reshape(count, block_size)
    previous = jnp.concatenate([jnp.reshape(before, (1,)), seg_blocks[:-1, -1]])

    def advance(carry_state, slab_in):
        q_blk, k_blk, v_blk, r_blk, s_blk, p_blk = slab_in
        return block_step(carry_state, q_blk, k_blk, v_blk, r_blk, s_blk, p_blk)

    start_state = jnp.zeros((heads_here, head_dim, head_dim), jnp.float32)
    final_state, block_outs = lax.scan(
        advance,
        start_state,
        (
            to_blocks(queries, count),
            to_blocks(key_rows, count),
            to_blocks(values_in, count),
            to_blocks(log_rates, count),
            seg_blocks,
            previous,
        ),
    )
    outputs = jnp.moveaxis(block_outs, 0, 1).reshape(heads_here, length, head_dim)
    return (outputs, final_state)


def local(latents, log_decay, seg_lengths, qkv_weight, out_weight, cotangent):
    strips, rate_strips = (
        lax.all_to_all(latents, "seq", split_axis=1, concat_axis=2, tiled=True),
        lax.all_to_all(log_decay, "seq", split_axis=1, concat_axis=2, tiled=True),
    )
    features = lax.all_gather(strips, "head", axis=3, tiled=True)
    proj_full, out_full = (
        lax.all_gather(qkv_weight, "seq", axis=0, tiled=True),
        lax.all_gather(out_weight, "seq", axis=0, tiled=True),
    )
    drives_here, rows_here, columns, feature_width = features.shape
    tokens_here = rows_here * columns
    heads_here = rate_strips.shape[3]
    head_dim = proj_full.shape[2] // heads_here
    block_size = min(512, tokens_here)
    split_weight = proj_full.reshape(feature_width, 3, heads_here, head_dim)
    projected = jnp.einsum(
        "bsaf,fchd->cbhsad", features, split_weight, preferred_element_type=jnp.float32
    ).astype(jnp.bfloat16)
    projected = projected.reshape(3, drives_here, heads_here, tokens_here, head_dim)
    log_rates = jnp.transpose(rate_strips.astype(jnp.float32), (0, 3, 1, 2)).reshape(
        drives_here, heads_here, tokens_here
    )
    starts = jnp.cumsum(seg_lengths, axis=1) - seg_lengths
    first_pos = lax.axis_index("seq") * tokens_here
    position = first_pos + jnp.arange(tokens_here, dtype=jnp.int32)
    segment = jnp.sum((starts[:, :, None] <= position[None, None, :]).astype(jnp.int32), axis=1) - 1
    before = jnp.sum((starts <= first_pos - 1).astype(jnp.int32), axis=1) - 1
    run_local = jax.vmap(partial(local_pass, block_size=block_size))
    local_out, own_state = run_local(
        projected[0], projected[1], projected[2], log_rates, segment, before
    )
    running = jnp.cumsum(log_rates, axis=2)
    joined_seg = (segment[:, -1] == before).astype(jnp.float32)
    self_decay = jnp.exp(running[:, :, -1]) * joined_seg[:, None]

    def relay(step_index, incoming):
        return shifted(self_decay[:, :, None, None] * incoming + own_state, "seq", 1)

    prefix = lax.fori_loop(0, lax.axis_size("seq") - 1, relay, jnp.zeros_like(own_state))
    head_scale = head_dim ** (-0.5)
    kept_mask = (segment == before[:, None]).astype(jnp.float32)
    carried = jnp.einsum(
        "bhtd,bhde->bhte", projected[0].astype(jnp.float32), prefix, precision=lax.Precision.HIGHEST
    )
    combined = (
        local_out
        + kept_mask[:, None, :, None] * jnp.exp(running)[:, :, :, None] * head_scale * carried
    )
    normed = combined * lax.rsqrt(jnp.mean(combined * combined, axis=-1, keepdims=True) + 1e-06)
    attn_rows = jnp.transpose(normed.astype(jnp.bfloat16), (0, 2, 1, 3)).reshape(
        drives_here * tokens_here, heads_here * head_dim
    )
    attn_full = lax.all_gather(attn_rows, "head", axis=1, tiled=True)
    layer_out = jnp.dot(attn_full, out_full, preferred_element_type=jnp.float32).astype(
        jnp.bfloat16
    )
    layer_out = layer_out.reshape(drives_here, rows_here, columns, out_full.shape[1])
    cot_rows = cotangent.reshape(drives_here * tokens_here, cotangent.shape[3])
    factor = float(lax.axis_size("dp") * lax.axis_size("seq") * drives_here * tokens_here) ** (-0.5)
    my_rows = lax.psum_scatter(
        lax.dot_general(
            attn_full, cot_rows, (((0,), (0,)), ((), ())), preferred_element_type=jnp.float32
        )
        * factor,
        "seq",
        scatter_dimension=0,
        tiled=True,
    )
    weight_grad = lax.psum(my_rows, "dp")
    return (layer_out, weight_grad)


def solution(mesh):
    in_specs = (
        P(("groups", "dp"), None, "seq", "head"),
        P(("groups", "dp"), None, "seq", "head"),
        P(("groups", "dp"), None),
        P("seq", None, "head"),
        P("seq", "head"),
        P(("groups", "dp"), "seq", None, "head"),
    )
    out_specs = (P(("groups", "dp"), "seq", None, "head"), P(("groups", "seq"), "head"))
    return jax.shard_map(local, mesh=mesh, in_specs=in_specs, out_specs=out_specs, check_vma=False)
```

profile of v0, /device:TPU:8, one launch (start us, length us, event | category | flops | bytes accessed | tf_op | source)
XLA Modules:
  0.0 308.7 jit_solution(2354458996665151048)
XLA Ops:
  7.2 0.7 all-gather.5.cloned.1.call-update
  8.0 52.7 %all_to_all.27 = bf16[1,8,128,512]{3,2,0,1:T(8,128)(2,1)S(1)} all-to-all(bf16[1,8,128,512]{3,2,0,1:T(8,128)(2,1)} %bitcast.208), channel_id=1, replica_groups=mesh['groups'=2,'seq'=4,'dp'=2,'head'=2] {'seq'}, dimensions={1} | all-to-all | bytes 2097152 | tf_op jit(solution)/shard_map/all_to_all | solution.py:79
  60.6 1.1 copy.67
  61.7 7.6 %all-to-all-start = ((bf16[1,8,128,4]{2,3,0,1:T(4,128)(2,1)}), bf16[1,8,128,4]{2,3,0,1:T(4,128)(2,1)S(1)}, u32[]{:S(2)}, u32[]{:S(2)}) async-start(bf16[1,8,128,4]{2,3,0,1:T(4,128)(2,1)} %bitcast.1), calls=%async_computation | async-start | bytes 16384 | tf_op jit(solution)/shard_map/all_to_all | solution.py:80
  69.5 0.6 fusion.38
  70.3 0.7 slice.57
  71.6 0.8 add_bitcast_fusion
  72.4 0.6 slice.64
  73.7 1.1 reduce-window.16
  75.8 10.8 %all-gather.5.cloned.1.call-done = bf16[1024,3,512]{2,0,1:T(8,128)(2,1)} async-done(((bf16[256,3,512]{2,0,1:T(8,128)(2,1)}), bf16[1024,3,512]{2,0,1:T(8,128)(2,1)}) %all-gather.5.cloned.1.call-update) | async-done | bytes 3145744 | tf_op jit(solution)/shard_map/all_gather | solution.py:84
  86.6 4.7 %copy.65 = bf16[1024,3,512]{0,2,1:T(8,128)(2,1)} copy(bf16[1024,3,512]{2,0,1:T(8,128)(2,1)} %all-gather.5.cloned.1.call-done) | data formatting | bytes 6291456 | tf_op jit(solution)/shard_map/all_gather | solution.py:84
  91.3 10.5 %all-gather.7.cloned.1.call-done = bf16[1,2,512,1024]{3,2,1,0:T(8,128)(2,1)} async-done(((bf16[1,2,512,512]{3,2,1,0:T(8,128)(2,1)}), bf16[1,2,512,1024]{3,2,1,0:T(8,128)(2,1)}) %all-gather.7.cloned.1.call-update) | async-done | bytes 2097168 | tf_op jit(solution)/shard_map/all_gather | solution.py:82
  101.8 6.1 %convert_bitcast_fusion = bf16[3,1,4,2,512,128]{4,5,3,2,0,1:T(8,128)(2,1)S(1)} fusion(bf16[1024,3,4,128,1]{0,3,4,2,1:T(8,128)(2,1)} %bitcast.204, bf16[1,2,512,1024]{3,2,1,0:T(8,128)(2,1)} %all-gather.7.cloned.1.call-done), kind=kOutput, calls=%fused_computation.48 | convolution fusion | flops 3222798336 | bytes 8388608 | tf_op jit(solution)/shard_map/bsaf,fchd->cbhsad/dot_general | solution.py:93
  107.9 2.2 fusion.41
  110.1 29.2 %while.24 = (s32[]{:T(128)}, f32[1,4,128,128]{3,2,1,0:T(8,128)S(1)}, f32[2,1,4,512,128]{4,3,2,1,0:T(8,128)}, f32[2,1,4,512]{3,2,1,0:T(4,128)S(1)}, s32[2,1,512]{...) while((s32[]{:T(128)}, ...), condition=%wide.region_6.7_spmd.clone, body=%wide.region_3.6_spmd.clone.sunk | while | flops 1015816256 | bytes 14092170 | solution.py:61
  111.3 1.2 reduce-window.26
  113.3 3.5 %fusion.69 = f32[4,512,128]{2,1,0:T(8,128)S(1)} fusion(f32[4,512]{1,0:T(4,128)S(1)} %get-tuple-element.263, pred[512,512]{1,0:T(8,128)(4,1)S(1)} %fusion.68, bf16[2,1,4,512,128]{3,4,0,2,1:T(8,128)(2,1)} %get-tuple-element.299, s32[]{:T(128)} %get-tuple-element.279, bf16[2,1,4,512,128]{3,4,0,2,1:T(8,128)(2,1)} %get-tuple-element.298, ...), kind=kOutput, calls=%fused_computation.2.clone.1 | convolution fusion | flops 543162368 | bytes 2901504 | tf_op jit(solution)/shard_map/vmap()/while/body/eval_jaxpr/hts,hsd->htd/dot_general | solution.py:25
  116.8 2.8 fusion.70
  119.7 0.6 slice.92
  121.6 0.6 compare_convert_fusion.7
  122.4 1.1 constant_dynamic-slice_fusion.10
  123.7 0.9 fusion.67
  125.9 1.2 reduce-window.26
  127.9 3.5 %fusion.69 = f32[4,512,128]{2,1,0:T(8,128)S(1)} fusion(f32[4,512]{1,0:T(4,128)S(1)} %get-tuple-element.263, pred[512,512]{1,0:T(8,128)(4,1)S(1)} %fusion.68, bf16[2,1,4,512,128]{3,4,0,2,1:T(8,128)(2,1)} %get-tuple-element.299, s32[]{:T(128)} %get-tuple-element.279, bf16[2,1,4,512,128]{3,4,0,2,1:T(8,128)(2,1)} %get-tuple-element.298, ...), kind=kOutput, calls=%fused_computation.2.clone.1 | convolution fusion | flops 543162368 | bytes 2901504 | tf_op jit(solution)/shard_map/vmap()/while/body/eval_jaxpr/hts,hsd->htd/dot_general | solution.py:25
  131.5 2.8 fusion.70
  134.3 0.6 slice.92
  136.2 0.6 compare_convert_fusion.7
  136.9 1.1 constant_dynamic-slice_fusion.10
  138.3 0.9 fusion.67
  139.3 2.9 copy.72
  142.1 2.9 reshape.615
  145.0 1.6 copy.76
  146.7 29.0 %while.23 = (s32[]{:T(128)}, f32[1,4,128,128]{3,2,1,0:T(8,128)S(1)}, f32[1,4]{1,0:T(1,128)S(1)}, f32[1,4,128,128]{3,2,1,0:T(8,128)S(1)}, s32[]{:T(128)}) while((s32[]{:T(128)}, f32[1,4,128,128]{3,2,1,0:T(8,128)S(1)}, f32[1,4]{1,0:T(1,128)S(1)}, f32[1,4,128,128]{3,2,1,0:T(8,128)S(1)}, s32[]{:T(128)}) %tuple.57), condition=%wide.region_10.11_spmd, body=%wide.region_9.10_spmd.sunk | while | flops 131074 | bytes 1835125 | solution.py:116
  146.8 3.4 %collective-permute-start = (f32[1,4,128,128]{3,2,1,0:T(8,128)S(1)}, f32[1,4,128,128]{3,2,1,0:T(8,128)S(1)}, u32[]{:S(2)}, u32[]{:S(2)}) collective-permute-start(f32[1,4,128,128]{3,2,1,0:T(8,128)S(1)} %multiply_add_fusion.3), channel_id=1, source_target_pairs={{0,4},{4,8},{8,12},{1,5},{5,9},{9,13},{2,6},{6,10},{10,14},{3,7},{... | collective-permute-start | bytes 786440 | tf_op jit(solution)/shard_map/while/body/eval_jaxpr/ppermute | solution.py:12
  150.2 7.0 %collective-permute-done = f32[1,4,128,128]{3,2,1,0:T(8,128)S(1)} collective-permute-done((f32[1,4,128,128]{3,2,1,0:T(8,128)S(1)}, f32[1,4,128,128]{3,2,1,0:T(8,128)S(1)}, u32[]{:S(2)}, u32[]{:S(2)}) %collective-permute-start) | collective-permute-done | bytes 262176 | tf_op jit(solution)/shard_map/while/body/eval_jaxpr/ppermute | solution.py:12
  157.3 3.4 %collective-permute-start = (f32[1,4,128,128]{3,2,1,0:T(8,128)S(1)}, f32[1,4,128,128]{3,2,1,0:T(8,128)S(1)}, u32[]{:S(2)}, u32[]{:S(2)}) collective-permute-start(f32[1,4,128,128]{3,2,1,0:T(8,128)S(1)} %multiply_add_fusion.3), channel_id=1, source_target_pairs={{0,4},{4,8},{8,12},{1,5},{5,9},{9,13},{2,6},{6,10},{10,14},{3,7},{... | collective-permute-start | bytes 786440 | tf_op jit(solution)/shard_map/while/body/eval_jaxpr/ppermute | solution.py:12
  160.7 6.2 %collective-permute-done = f32[1,4,128,128]{3,2,1,0:T(8,128)S(1)} collective-permute-done((f32[1,4,128,128]{3,2,1,0:T(8,128)S(1)}, f32[1,4,128,128]{3,2,1,0:T(8,128)S(1)}, u32[]{:S(2)}, u32[]{:S(2)}) %collective-permute-start) | collective-permute-done | bytes 262176 | tf_op jit(solution)/shard_map/while/body/eval_jaxpr/ppermute | solution.py:12
  167.0 3.4 %collective-permute-start = (f32[1,4,128,128]{3,2,1,0:T(8,128)S(1)}, f32[1,4,128,128]{3,2,1,0:T(8,128)S(1)}, u32[]{:S(2)}, u32[]{:S(2)}) collective-permute-start(f32[1,4,128,128]{3,2,1,0:T(8,128)S(1)} %multiply_add_fusion.3), channel_id=1, source_target_pairs={{0,4},{4,8},{8,12},{1,5},{5,9},{9,13},{2,6},{6,10},{10,14},{3,7},{... | collective-permute-start | bytes 786440 | tf_op jit(solution)/shard_map/while/body/eval_jaxpr/ppermute | solution.py:12
  170.4 5.3 %collective-permute-done = f32[1,4,128,128]{3,2,1,0:T(8,128)S(1)} collective-permute-done((f32[1,4,128,128]{3,2,1,0:T(8,128)S(1)}, f32[1,4,128,128]{3,2,1,0:T(8,128)S(1)}, u32[]{:S(2)}, u32[]{:S(2)}) %collective-permute-start) | collective-permute-done | bytes 262176 | tf_op jit(solution)/shard_map/while/body/eval_jaxpr/ppermute | solution.py:12
  175.6 2.9 multiply_reduce_fusion
  178.5 1.2 multiply_convert_fusion.3
  179.9 11.8 %all-gather.9.cloned.1.call-done = bf16[1024,1024]{0,1:T(8,128)(2,1)} async-done(((bf16[1024,512]{0,1:T(8,128)(2,1)}), bf16[1024,1024]{0,1:T(8,128)(2,1)}) %all-gather.9.cloned.1.call-update) | async-done | bytes 2097168 | tf_op jit(solution)/shard_map/all_gather | solution.py:130
  191.7 4.1 %convolution_multiply_fusion.1 = f32[1024,512]{1,0:T(8,128)} fusion(bf16[1024,1024]{0,1:T(8,128)(2,1)} %all-gather.9.cloned.1.call-done, bf16[1024,512]{1,0:T(8,128)(2,1)S(1)} %bitcast.196), kind=kOutput, calls=%fused_computation.53 | convolution fusion | flops 1074266112 | bytes 5242880 | tf_op jit(solution)/shard_map/dot_general | solution.py:138
  196.5 42.0 %reduce-scatter.2.cloned.1.call-done = f32[256,512]{1,0:T(8,128)} async-done(((f32[1024,512]{1,0:T(8,128)}), f32[256,512]{1,0:T(8,128)}) %reduce-scatter.2.cloned.1.call-update) | async-done | bytes 524304 | tf_op jit(solution)/shard_map/reduce_scatter | solution.py:137
  238.6 31.0 %all-gather.11.cloned.1.call-done = bf16[1024,512]{1,0:T(8,128)(2,1)} async-done(((bf16[256,512]{1,0:T(8,128)(2,1)}), bf16[1024,512]{1,0:T(8,128)(2,1)}) %all-gather.11.cloned.1.call-update) | async-done | bytes 1048592 | tf_op jit(solution)/shard_map/all_gather | solution.py:85
  269.5 3.5 %convolution_convert_fusion = bf16[1024,512]{1,0:T(8,128)(2,1)} fusion(bf16[1024,1024]{0,1:T(8,128)(2,1)S(1)} %copy-done.3, bf16[1024,512]{1,0:T(8,128)(2,1)} %all-gather.11.cloned.1.call-done), kind=kOutput, calls=%fused_computation.54 | convolution fusion | flops 1074266112 | bytes 4194304 | tf_op jit(solution)/shard_map/dot_general | solution.py:131
  273.0 26.9 %all-reduce.2.cloned.1.call-done = f32[256,512]{1,0:T(8,128)} async-done(((f32[256,512]{1,0:T(8,128)}), f32[256,512]{1,0:T(8,128)}) %all-reduce.2.cloned.1.call-update) | async-done | bytes 524304 | tf_op jit(solution)/shard_map/psum | solution.py:146
  299.9 1.9 copy.123
  (85 shorter events, 7.4 us)
Async XLA Ops:
  7.2 184.5 %copy-start = (bf16[1,2,512,512]{3,2,1,0:T(8,128)(2,1)S(1)}, bf16[1,2,512,512]{3,2,1,0:T(8,128)(2,1)}, u32[]{:S(2)}) copy-start(bf16[1,2,512,512]{3,2,1,0:T(8,128)(2,1)} %param.15) | copy-start | bytes 3145732
  7.2 79.4 %all-gather.5.cloned.1.call-start = ((), (), s32[]{:S(2)}) async-start(), calls=%async_computation.3 | async-start | bytes 3932160 | tf_op jit(solution)/shard_map/all_gather | solution.py:84
  7.9 93.9 %all-gather.7.cloned.1.call-start = ((), (), s32[]{:S(2)}) async-start(), calls=%async_computation.4 | async-start | bytes 3145728 | tf_op jit(solution)/shard_map/all_gather | solution.py:82
  60.6 8.7 %copy-start.2 = (s32[1,4]{1,0:T(1,128)S(1)}, s32[1,4]{1,0:T(1,128)}, u32[]{:S(2)}) copy-start(s32[1,4]{1,0:T(1,128)} %param.12) | copy-start | bytes 52
  61.7 11.9 %all-to-all-start = ((bf16[1,8,128,4]{2,3,0,1:T(4,128)(2,1)}), bf16[1,8,128,4]{2,3,0,1:T(4,128)(2,1)S(1)}, u32[]{:S(2)}, u32[]{:S(2)}) async-start(bf16[1,8,128,4]{2,3,0,1:T(4,128)(2,1)} %bitcast.1), calls=%async_computation | async-start | bytes 16384 | tf_op jit(solution)/shard_map/all_to_all | solution.py:80
  69.4 122.4 %all-gather.9.cloned.1.call-start = ((), (), s32[]{:S(2)}) async-start(), calls=%async_computation.5 | async-start | bytes 3145728 | tf_op jit(solution)/shard_map/all_gather | solution.py:130
  119.7 4.1 %copy-start.1 = (bf16[2,1,4,512,128]{3,4,0,2,1:T(8,128)(2,1)S(1)}, bf16[2,1,4,512,128]{3,4,0,2,1:T(8,128)(2,1)}, u32[]{:S(2)}) copy-start(bf16[2,1,4,512,128]{3,4,0,2,1:T(8,128)(2,1)} %get-tuple-element.298) | copy-start | bytes 3145732 | tf_op jit(solution)/shard_map/vmap()/while
  134.3 4.1 %copy-start.1 = (bf16[2,1,4,512,128]{3,4,0,2,1:T(8,128)(2,1)S(1)}, bf16[2,1,4,512,128]{3,4,0,2,1:T(8,128)(2,1)}, u32[]{:S(2)}) copy-start(bf16[2,1,4,512,128]{3,4,0,2,1:T(8,128)(2,1)} %get-tuple-element.298) | copy-start | bytes 3145732 | tf_op jit(solution)/shard_map/vmap()/while
  146.8 10.4 %collective-permute-start = (f32[1,4,128,128]{3,2,1,0:T(8,128)S(1)}, f32[1,4,128,128]{3,2,1,0:T(8,128)S(1)}, u32[]{:S(2)}, u32[]{:S(2)}) collective-permute-start(f32[1,4,128,128]{3,2,1,0:T(8,128)S(1)} %multiply_add_fusion.3), channel_id=1, source_target_pairs={{0,4},{4,8},{8,12},{1,5},{5,9},{9,13},{2,6},{6,10},{10,14},{3,7},{... | collective-permute-start | bytes 786440 | tf_op jit(solution)/shard_map/while/body/eval_jaxpr/ppermute | solution.py:12
  157.3 9.6 %collective-permute-start = (f32[1,4,128,128]{3,2,1,0:T(8,128)S(1)}, f32[1,4,128,128]{3,2,1,0:T(8,128)S(1)}, u32[]{:S(2)}, u32[]{:S(2)}) collective-permute-start(f32[1,4,128,128]{3,2,1,0:T(8,128)S(1)} %multiply_add_fusion.3), channel_id=1, source_target_pairs={{0,4},{4,8},{8,12},{1,5},{5,9},{9,13},{2,6},{6,10},{10,14},{3,7},{... | collective-permute-start | bytes 786440 | tf_op jit(solution)/shard_map/while/body/eval_jaxpr/ppermute | solution.py:12
  167.0 8.7 %collective-permute-start = (f32[1,4,128,128]{3,2,1,0:T(8,128)S(1)}, f32[1,4,128,128]{3,2,1,0:T(8,128)S(1)}, u32[]{:S(2)}, u32[]{:S(2)}) collective-permute-start(f32[1,4,128,128]{3,2,1,0:T(8,128)S(1)} %multiply_add_fusion.3), channel_id=1, source_target_pairs={{0,4},{4,8},{8,12},{1,5},{5,9},{9,13},{2,6},{6,10},{10,14},{3,7},{... | collective-permute-start | bytes 786440 | tf_op jit(solution)/shard_map/while/body/eval_jaxpr/ppermute | solution.py:12
  179.8 58.7 %reduce-scatter.2.cloned.1.call-start = ((), (), s32[]{:S(2)}) async-start(), calls=%async_computation.7 | async-start | bytes 2621440 | tf_op jit(solution)/shard_map/reduce_scatter | solution.py:137
  195.8 73.7 %copy-start.3 = (bf16[1024,1024]{0,1:T(8,128)(2,1)S(1)}, bf16[1024,1024]{0,1:T(8,128)(2,1)}, u32[]{:S(2)}) copy-start(bf16[1024,1024]{0,1:T(8,128)(2,1)} %all-gather.9.cloned.1.call-done) | copy-start | bytes 6291460
  195.9 73.7 %all-gather.11.cloned.1.call-start = ((), (), s32[]{:S(2)}) async-start(), calls=%async_computation.6 | async-start | bytes 1310720 | tf_op jit(solution)/shard_map/all_gather | solution.py:85
  196.5 103.5 %all-reduce.2.cloned.1.call-start = ((), (), s32[]{:S(2)}) async-start(), calls=%async_computation.8 | async-start | bytes 1048576 | tf_op jit(solution)/shard_map/psum | solution.py:146
Sparse Core Ops, SparseCore 0:
  9.6 76.9 all-gather.4
  88.7 13.0 all-gather.6
  179.9 11.7 all-gather.8
  196.0 42.4 reduce-scatter.1
  240.0 29.4 all-gather.10
  271.8 28.1 all-reduce.1
where the time goes:
time: 311 us; the launch traced here: 309 us
  waiting for transfers between devices  153 us (49%)
  blocking collectives  52.7 us (17%)
  matrix products  31.1 us (10%)
  local copies, waits for them, and re-layouts  25.4 us (8%)
  starting transfers between devices  18 us (6%)
  between operations  15.5 us (5%)
  other arithmetic  10.4 us (3%)
    all_to_all x1, blocking collectives, local(): lax.all_to_all(latents, 'seq', split_axis=1, concat_axis=2, tiled=True)  52.7 us
    reduce_scatter x1, waiting for transfers between devices, local(): lax.psum_scatter(lax.dot_general(attn_full, cot_rows, (((0,), (0,)), ((),...  42 us
    all_gather x1, waiting for transfers between devices, local(): lax.all_gather(out_weight, 'seq', axis=0, tiled=True)  31 us
    psum x1, waiting for transfers between devices, local(): weight_grad = lax.psum(my_rows, 'dp')  26.9 us
    ppermute x3, waiting for transfers between devices, shifted(): lax.ppermute(value, axis, [(source, source + steps) for source in range(i...  18.5 us
    all_gather x1, waiting for transfers between devices, local(): attn_full = lax.all_gather(attn_rows, 'head', axis=1, tiled=True)  11.8 us
    all_gather x1, waiting for transfers between devices, local(): lax.all_gather(qkv_weight, 'seq', axis=0, tiled=True)  10.8 us
    all_gather x1, waiting for transfers between devices, local(): features = lax.all_gather(strips, 'head', axis=3, tiled=True)  10.5 us
  transfers between devices with their start and end apart: 10, of which 10 were waited for; matrix products, arithmetic and copies ran while one was open for 5% of the time, Pallas kernels for 0%

commit v1 on v0

v1 whole, which is shorter than its diff:
```python
from functools import partial

import jax
import jax.numpy as jnp
from jax import lax
from jax.experimental import pallas as pl
from jax.experimental.pallas import tpu as pltpu

BF = jnp.bfloat16
F32 = jnp.float32


def remote(src, dst, send, recv, device):
    return pltpu.make_async_remote_copy(
        src_ref=src,
        dst_ref=dst,
        send_sem=send,
        recv_sem=recv,
        device_id=device,
        device_id_type=pl.DeviceIdType.MESH,
    )


def dot(a, b, ca=1, cb=0, **kw):
    return lax.dot_general(
        a, b, (((ca,), (cb,)), ((), ())), preferred_element_type=F32, **kw
    )


def kernel(
    n, dpn, chunk,
    seg, lat, rates, wqkv, wout, cot,
    out, grad,
    xbuf, wbuf, obuf, cotv, ldr, cumr, cumb, kv, intra, states, gains, mine, totals,
    sbuf, tbuf, attn, gsend, grecv, gdp, gdr,
    loc, xs, xr, xfs, xfr, ws, wr, wfs, wfr, lds, ldrs, ss, sr, ts, tr, ats, atr,
    gs, gr, ds_, dr,
):
    z = lax.axis_index("seq")
    h = lax.axis_index("head")
    d = lax.axis_index("dp")
    g = lax.axis_index("groups")
    rows, width = xbuf.shape[1], xbuf.shape[2]
    strip = lat.shape[1]
    half = xbuf.shape[3]
    tokens = rows * width
    heads = half // 128
    per_row = width // chunk
    chunks = rows * per_row
    shard = wout.shape[0]
    piece = shard // 4
    scale = 128 ** (-0.5)
    quarter = (d % 2) * 2 + g
    pair = d + 1 - 2 * (d % 2)
    partners = ({"dp": pair}, {"groups": 1 - g}, {"dp": pair, "groups": 1 - g})

    barrier = pltpu.get_barrier_semaphore()
    count = 0
    for device in (
        [{"seq": lax.rem(z + o, n)} for o in range(1, n)]
        + [{"head": 1 - h}, {"groups": 1 - g}, {"dp": pair, "groups": 1 - g}]
        + [{"dp": lax.rem(d + o, dpn)} for o in range(1, dpn)]
    ):
        pl.semaphore_signal(
            barrier, inc=1, device_id=device, device_id_type=pl.DeviceIdType.MESH
        )
        count += 1
    pl.semaphore_wait(barrier, count)

    def to(o):
        return lax.rem(z + o, n)

    def frm(o):
        return lax.rem(z + n - o, n)

    def mult(v, m):
        return pl.multiple_of(v, m)

    def xslot(src):
        return xbuf.at[h, :, pl.ds(mult(src * strip, strip), strip), :]

    def xslot_other(src):
        return xbuf.at[1 - h, :, pl.ds(mult(src * strip, strip), strip), :]

    def lat_block(dst):
        return lat.at[pl.ds(dst * rows, rows)]

    sent = []
    for o in range(1, n):
        c = remote(rates.at[to(o)], ldr.at[z], lds.at[o - 1], ldrs.at[o - 1], {"seq": to(o)})
        c.start()
        sent.append(c)
    local = [
        pltpu.make_async_copy(rates.at[z], ldr.at[z], loc.at[0]),
        pltpu.make_async_copy(lat_block(z), xslot(z), loc.at[1]),
        pltpu.make_async_copy(wqkv, wbuf.at[:, pl.ds(mult(z * shard, shard), shard), :], loc.at[2]),
        pltpu.make_async_copy(wout, obuf.at[pl.ds(mult(z * shard, shard), shard), :], loc.at[3]),
        pltpu.make_async_copy(cot, cotv, loc.at[4]),
    ]
    for o in range(1, n):
        c = remote(lat_block(to(o)), xslot(z), xs.at[o - 1], xr.at[o - 1], {"seq": to(o)})
        c.start()
        sent.append(c)

    def wsrc(a, row):
        rng = pl.ds(mult(row, piece), piece)
        return (wqkv.at[pl.ds(1, 2), rng, :], wqkv.at[0, rng, :], wout.at[rng, :])[a]

    def wdst(a, row):
        rng = pl.ds(mult(row, piece), piece)
        return (wbuf.at[pl.ds(1, 2), rng, :], wbuf.at[0, rng, :], obuf.at[rng, :])[a]

    for a in range(3):
        for o in range(1, n):
            c = remote(
                wsrc(a, quarter * piece), wdst(a, z * shard + quarter * piece),
                ws.at[a, o - 1], wr.at[a, o - 1], {"seq": to(o)},
            )
            c.start()
            sent.append(c)
    own = remote(lat_block(z), xslot(z), xfs.at[0], xfr.at[0], {"head": 1 - h})
    own.start()
    sent.append(own)
    for c in local:
        c.start()

    local[0].wait()
    for o in range(1, n):
        remote(rates.at[z], ldr.at[frm(o)], lds.at[o - 1], ldrs.at[o - 1], {"seq": frm(o)}).wait_recv()
    rate = ldr[0]
    for i in range(1, n):
        rate = rate + ldr[i]
    row_i = lax.broadcasted_iota(jnp.int32, (chunk, chunk), 0)
    col_i = lax.broadcasted_iota(jnp.int32, (chunk, chunk), 1)
    upper = jnp.where(row_i <= col_i, 1.0, 0.0).astype(F32)
    lower = jnp.where(row_i >= col_i, 1.0, 0.0).astype(F32)
    for j in range(per_row):
        part = rate[:, j * chunk:(j + 1) * chunk]
        cumr[:, j * chunk:(j + 1) * chunk] = dot(part, upper, precision=lax.Precision.HIGHEST)
        cumc = dot(lower, part, 1, 1, precision=lax.Precision.HIGHEST)
        for i in range(rows * heads):
            cumb[i, j * chunk:(j + 1) * chunk, :] = jnp.broadcast_to(cumc[:, i:i + 1], (chunk, 128))

    for o in range(1, n):
        remote(lat_block(z), xslot(frm(o)), xs.at[o - 1], xr.at[o - 1], {"seq": frm(o)}).wait_recv()
        c = remote(xslot(frm(o)), xslot(frm(o)), xfs.at[o], xfr.at[o], {"head": 1 - h})
        c.start()
        sent.append(c)

    def forward(a):
        for o in range(1, n):
            slot = wdst(a, frm(o) * shard + quarter * piece)
            remote(wsrc(a, quarter * piece), slot, ws.at[a, o - 1], wr.at[a, o - 1], {"seq": frm(o)}).wait_recv()
            for p in range(3):
                c = remote(slot, slot, wfs.at[a, o - 1, p], wfr.at[a, o - 1, p], partners[p])
                c.start()
                sent.append(c)

    other_quarter = (
        (1 - d % 2) * 2 + g, (d % 2) * 2 + 1 - g, (1 - d % 2) * 2 + 1 - g
    )

    def forwarded(a):
        for o in range(1, n):
            for p in range(3):
                slot = wdst(a, frm(o) * shard + other_quarter[p] * piece)
                remote(slot, slot, wfs.at[a, o - 1, p], wfr.at[a, o - 1, p], partners[p]).wait_recv()

    forward(0)
    forward(1)
    local[1].wait()
    local[2].wait()
    for o in range(n):
        src = z if o == 0 else frm(o)
        remote(xslot_other(src), xslot_other(src), xfs.at[o], xfr.at[o], {"head": 1 - h}).wait_recv()
    forwarded(0)

    def project(c):
        def step(i, carry):
            r, j = i // per_row, i % per_row
            at = pl.ds(mult(j * chunk, chunk), chunk)
            acc = dot(xbuf[0, r, at, :], wbuf[c, :half, :]) + dot(xbuf[1, r, at, :], wbuf[c, half:, :])
            kv[c, pl.ds(mult(i * chunk, chunk), chunk), :] = acc.astype(BF)
            return carry

        lax.fori_loop(0, chunks, step, 0)

    project(1)
    project(2)

    starts = [jnp.int32(0)]
    for j in range(seg.shape[1] - 1):
        starts.append(starts[-1] + seg[0, j])

    def seg_at(position):
        total = jnp.int32(-1)
        for s in starts:
            total = total + jnp.where(s <= position, 1, 0)
        return total

    def seg_vec(position):
        total = jnp.full(position.shape, -1, jnp.int32)
        for s in starts:
            total = total + jnp.where(position >= s, 1, 0)
        return total

    first = z * tokens
    tall = lax.broadcasted_iota(jnp.int32, (chunk, 128), 0)

    def state_head(hh, carry):
        lanes = pl.ds(mult(hh * 128, 128), 128)
        state = jnp.zeros((128, 128), F32)
        gain = jnp.ones((1, 128), F32)
        for ci in range(chunks):
            r, j = ci // per_row, ci % per_row
            base = first + ci * chunk
            cum = cumb[r * heads + hh, j * chunk:(j + 1) * chunk, :]
            last = cumb[r * heads + hh, (j + 1) * chunk - 1:(j + 1) * chunk, :]
            seg_last = seg_at(base + chunk - 1)
            tail = jnp.where(seg_vec(tall + base) == seg_last, jnp.exp(last - cum), 0.0)
            toks = pl.ds(ci * chunk, chunk)
            dk = (kv[1, toks, lanes].astype(F32) * tail).astype(BF)
            fresh = dot(dk, kv[2, toks, lanes], 0, 0)
            states[hh, ci] = state
            gains[hh, ci:ci + 1, :] = gain
            through = jnp.exp(last) * jnp.where(seg_last == seg_at(base - 1), 1.0, 0.0)
            state = state * through + fresh
            gain = gain * through
        mine[pl.ds(mult(hh * 128, 128), 128), :] = state.astype(BF)
        totals[pl.ds(hh * 8, 8), :] = jnp.broadcast_to(gain, (8, 128))
        return carry

    lax.fori_loop(0, heads, state_head, 0)

    for o in range(1, n):
        @pl.when(z + o < n)
        def _():
            remote(mine, sbuf.at[o - 1], ss.at[o - 1], sr.at[o - 1], {"seq": z + o}).start()
            remote(totals, tbuf.at[o - 1], ts.at[o - 1], tr.at[o - 1], {"seq": z + o}).start()

    forward(2)
    forwarded(1)
    project(0)

    def within(idx, carry):
        hh, ci = idx // chunks, idx % chunks
        r, j = ci // per_row, ci % per_row
        lanes = pl.ds(mult(hh * 128, 128), 128)
        toks = pl.ds(mult(ci * chunk, chunk), chunk)
        at = pl.ds(mult(j * chunk, chunk), chunk)
        base = first + ci * chunk
        cum = cumb[r * heads + hh, at, :]
        column = jnp.concatenate([cum] * (chunk // 128), axis=1)
        row = cumr[pl.ds(r * heads + hh, 1), at]
        seg_row = seg_vec(base + lax.broadcasted_iota(jnp.int32, (1, chunk), 1))
        seg_col = seg_vec(base + lax.broadcasted_iota(jnp.int32, (chunk, 1), 0))
        allowed = (row_i >= col_i) & (seg_col == seg_row)
        weight = jnp.where(allowed, jnp.exp(jnp.where(allowed, column - row, 0.0)), 0.0)
        scores = dot(kv[0, toks, lanes], kv[1, toks, lanes], 1, 1)
        mixing = (scores * scale * weight).astype(BF)
        intra[toks, lanes] = dot(mixing, kv[2, toks, lanes])
        return carry

    lax.fori_loop(0, heads * chunks, within, 0)

    for o in range(1, n):
        @pl.when(z + o < n)
        def _():
            remote(mine, sbuf.at[o - 1], ss.at[o - 1], sr.at[o - 1], {"seq": z + o}).wait_send()
            remote(totals, tbuf.at[o - 1], ts.at[o - 1], tr.at[o - 1], {"seq": z + o}).wait_send()
    for hh in range(heads):
        states[hh, chunks] = jnp.zeros((128, 128), F32)
    for o in range(n - 1, 0, -1):
        @pl.when(z - o >= 0)
        def _():
            remote(mine, sbuf.at[o - 1], ss.at[o - 1], sr.at[o - 1], {"seq": z - o}).wait_recv()
            remote(totals, tbuf.at[o - 1], ts.at[o - 1], tr.at[o - 1], {"seq": z - o}).wait_recv()
            for hh in range(heads):
                states[hh, chunks] = (
                    states[hh, chunks] * tbuf[o - 1, hh * 8:hh * 8 + 1, :]
                    + sbuf[o - 1, hh * 128:(hh + 1) * 128, :].astype(F32)
                )

    def finish(hh):
        lanes = pl.ds(hh * 128, 128)

        def step(ci, carry):
            r, j = ci // per_row, ci % per_row
            toks = pl.ds(mult(ci * chunk, chunk), chunk)
            base = first + ci * chunk
            cum = cumb[r * heads + hh, pl.ds(mult(j * chunk, chunk), chunk), :]
            state = states[hh, ci] + gains[hh, pl.ds(ci, 1), :] * states[hh, chunks]
            carried = dot(kv[0, toks, lanes], state.astype(BF))
            kept = jnp.where(seg_vec(tall + base) == seg_at(base - 1), jnp.exp(cum), 0.0)
            o = intra[toks, lanes] + kept * carried * scale
            norm = lax.rsqrt(jnp.mean(o * o, axis=1, keepdims=True) + 1e-6)
            attn[h, toks, lanes] = (o * norm).astype(BF)
            return carry

        lax.fori_loop(0, chunks, step, 0)

    for hh in range(heads):
        finish(hh)
        lanes = pl.ds(hh * 128, 128)
        c = remote(attn.at[h, :, lanes], attn.at[h, :, lanes], ats.at[hh], atr.at[hh], {"head": 1 - h})
        c.start()
        sent.append(c)

    local[4].wait()
    factor = float(dpn * n * tokens) ** (-0.5)

    def grad_half(which):
        def step(i, carry):
            lanes = pl.ds(mult(i * 128, 128), 128)
            part = dot(attn[which, :, lanes], cotv[...], 0, 0) * factor
            gsend[pl.ds(mult(which * half + i * 128, 128), 128), :] = part.astype(BF)
            return carry

        lax.fori_loop(0, heads, step, 0)

    grad_half(h)
    for hh in range(heads):
        lanes = pl.ds(hh * 128, 128)
        remote(attn.at[1 - h, :, lanes], attn.at[1 - h, :, lanes], ats.at[hh], atr.at[hh], {"head": 1 - h}).wait_recv()
    grad_half(1 - h)
    for o in range(1, n):
        c = remote(
            gsend.at[pl.ds(mult(to(o) * shard, shard), shard), :], grecv.at[o - 1],
            gs.at[o - 1], gr.at[o - 1], {"seq": to(o)},
        )
        c.start()
        sent.append(c)

    local[3].wait()
    forwarded(2)

    def out_step(i, carry):
        toks = pl.ds(mult(i * chunk, chunk), chunk)
        acc = dot(attn[0, toks, :], obuf[:half, :]) + dot(attn[1, toks, :], obuf[half:, :])
        out[toks, :] = acc.astype(BF)
        return carry

    lax.fori_loop(0, chunks, out_step, 0)

    total = gsend[pl.ds(mult(z * shard, shard), shard), :].astype(F32)
    for o in range(1, n):
        remote(gsend.at[pl.ds(0, shard), :], grecv.at[o - 1], gs.at[o - 1], gr.at[o - 1], {"seq": frm(o)}).wait_recv()
        total = total + grecv[o - 1].astype(F32)
    gdp[...] = total.astype(BF)
    gdr[d] = gdp[...]
    for o in range(1, dpn):
        peer = lax.rem(d + o, dpn)
        c = remote(gdp, gdr.at[d], ds_.at[o - 1], dr.at[o - 1], {"dp": peer})
        c.start()
        sent.append(c)
    for o in range(1, dpn):
        peer = lax.rem(d + dpn - o, dpn)
        remote(gdp, gdr.at[peer], ds_.at[o - 1], dr.at[o - 1], {"dp": peer}).wait_recv()
    total = gdr[0].astype(F32)
    for i in range(1, dpn):
        total = total + gdr[i].astype(F32)
    grad[...] = total
    for c in sent:
        c.wait_send()


def local(n, dpn, latents, log_decay, seg_lengths, qkv_weight, out_weight, cotangent):
    _, all_rows, strip, half = latents.shape
    rows = all_rows // n
    width = strip * n
    tokens = rows * width
    heads = log_decay.shape[3]
    shard = out_weight.shape[0]
    chunk = min(256, width)
    chunks = tokens // chunk
    z = lax.axis_index("seq")
    rates = jnp.transpose(log_decay[0].astype(F32), (0, 2, 1)).reshape(n, rows * heads, strip)
    column = lax.broadcasted_iota(jnp.int32, (1, 1, width), 2)
    rates = jnp.where(column // strip == z, jnp.tile(rates, (1, 1, n)), 0.0)
    wqkv = jnp.transpose(qkv_weight, (1, 0, 2))
    anyspace = pl.BlockSpec(memory_space=pl.ANY)
    vmem = pl.BlockSpec(memory_space=pltpu.VMEM)
    dma = pltpu.SemaphoreType.DMA
    m = n - 1
    out, grad = pl.pallas_call(
        partial(kernel, n, dpn, chunk),
        out_shape=(
            jax.ShapeDtypeStruct((tokens, half), BF),
            jax.ShapeDtypeStruct((shard, half), F32),
        ),
        in_specs=[pl.BlockSpec(memory_space=pltpu.SMEM)] + [anyspace] * 5,
        out_specs=(vmem, vmem),
        scratch_shapes=[
            pltpu.VMEM((2, rows, width, half), BF),
            pltpu.VMEM((3, 2 * half, half), BF),
            pltpu.VMEM((2 * half, half), BF),
            pltpu.VMEM((tokens, half), BF),
            pltpu.VMEM((n, rows * heads, width), F32),
            pltpu.VMEM((rows * heads, width), F32),
            pltpu.VMEM((rows * heads, width, 128), F32),
            pltpu.VMEM((3, tokens, half), BF),
            pltpu.VMEM((tokens, half), F32),
            pltpu.VMEM((heads, chunks + 1, 128, 128), F32),
            pltpu.VMEM((heads, chunks, 128), F32),
            pltpu.VMEM((half, 128), BF),
            pltpu.VMEM((heads * 8, 128), F32),
            pltpu.VMEM((m, half, 128), BF),
            pltpu.VMEM((m, heads * 8, 128), F32),
            pltpu.VMEM((2, tokens, half), BF),
            pltpu.VMEM((2 * half, half), BF),
            pltpu.VMEM((m, shard, half), BF),
            pltpu.VMEM((shard, half), BF),
            pltpu.VMEM((dpn, shard, half), BF),
            dma((5,)),
            dma((m,)), dma((m,)), dma((n,)), dma((n,)),
            dma((3, m)), dma((3, m)), dma((3, m, 3)), dma((3, m, 3)),
            dma((m,)), dma((m,)),
            dma((m,)), dma((m,)), dma((m,)), dma((m,)),
            dma((heads,)), dma((heads,)),
            dma((m,)), dma((m,)),
            dma((dpn - 1,)), dma((dpn - 1,)),
        ],
        compiler_params=pltpu.CompilerParams(
            collective_id=0, has_side_effects=True, vmem_limit_bytes=56 * 1024 * 1024
        ),
    )(
        seg_lengths, latents[0], rates, wqkv, out_weight,
        cotangent.reshape(tokens, half),
    )
    return out.reshape(1, rows, width, half), grad


def solution(mesh):
    from jax.sharding import PartitionSpec as P

    in_specs = (
        P(("groups", "dp"), None, "seq", "head"),
        P(("groups", "dp"), None, "seq", "head"),
        P(("groups", "dp"), None),
        P("seq", None, "head"),
        P("seq", "head"),
        P(("groups", "dp"), "seq", None, "head"),
    )
    out_specs = (P(("groups", "dp"), "seq", None, "head"), P(("groups", "seq"), "head"))
    return jax.shard_map(
        partial(local, mesh.shape["seq"], mesh.shape["dp"]),
        mesh=mesh, in_specs=in_specs, out_specs=out_specs, check_vma=False,
    )
```

time: 311 us -> 126 us (0.41)
  waiting for transfers between devices: 153 us -> 0 us
  Pallas kernels: 0 us -> 120 us
  blocking collectives: 52.7 us -> 0 us
  matrix products: 31.1 us -> 0 us
  local copies, waits for them, and re-layouts: 25.4 us -> 3.79 us
  starting transfers between devices: 18 us -> 0 us
  between operations: 15.5 us -> 0.67 us
  other arithmetic: 10.4 us -> 0.65 us
    pallas_call x0 -> x1, Pallas kernels: none -> 120 us  [local(): pl.pallas_call(partial(kernel, n, dpn, chunk), out_shape=(jax.ShapeDtypeS...]
    all_gather x4 -> x0, waiting for transfers between devices: 64.2 us -> none  [the longest x1 31 us: local(): lax.all_gather(out_weight, 'seq', axis=0, tiled=True)]
    all_to_all x1 -> x0, blocking collectives: 52.7 us -> none  [local(): lax.all_to_all(latents, 'seq', split_axis=1, concat_axis=2, tiled=True)]
    reduce_scatter x1 -> x0, waiting for transfers between devices: 42 us -> none  [local(): lax.psum_scatter(lax.dot_general(attn_full, cot_rows, (((0,), (0,)), ((),...]
    dot_general x10 -> x0, matrix products: 31.1 us -> none  [the longest x2 7.05 us: block_step(): jnp.einsum('hts,hsd->htd', mixing, values_in, preferred_element_type=jnp....]
    psum x1 -> x0, waiting for transfers between devices: 26.9 us -> none  [local(): weight_grad = lax.psum(my_rows, 'dp')]
    ppermute x3 -> x0, waiting for transfers between devices: 18.5 us -> none  [shifted(): lax.ppermute(value, axis, [(source, source + steps) for source in range(i...]
    ppermute x3 -> x0, starting transfers between devices: 10.2 us -> none  [shifted(): lax.ppermute(value, axis, [(source, source + steps) for source in range(i...]
  transfers between devices with their start and end apart: 10 -> 0, of which waited for: 10 -> 0; matrix products, arithmetic and copies ran while one was open for 5% -> 0% of each run, Pallas kernels for 0% -> 0%
where the time goes in v1:
time: 126 us; the launch traced here: 125 us
  Pallas kernels  120 us (95%)
  local copies, waits for them, and re-layouts  3.79 us (3%)
    pallas_call x1, Pallas kernels, local(): pl.pallas_call(partial(kernel, n, dpn, chunk), out_shape=(jax.ShapeDtypeS...  120 us
    unnamed x6, local copies, waits for them, and re-layouts  3.79 us

profile of v1, /device:TPU:8, one launch (start us, length us, event | category | flops | bytes accessed | tf_op | source)
XLA Modules:
  0.0 125.3 jit_solution(1905748869007424786)
XLA Ops:
  0.6 0.0 copy-start.1
  0.7 0.7 copy-done.1
  1.3 0.6 bitcast_select_fusion.rates
  2.0 120.2 %shard_map.77 = (bf16[1024,512]{1,0:T(8,128)(2,1)}, f32[256,512]{1,0:T(8,128)}) custom-call(s32[1,4]{1,0:T(1,128)} %seg.1, bf16[8,128,512]{2,1,0:T(8,128)(2,1)} %bitcast.12, f32[4,8,512]{2,1,0:T(8,128)} %bitcast_select_fusion.rates, bf16[3,256,512]{2,1,0:T(8,128)(2,1)} %bitcast.15, bf16[256,512]{1,0:T(8,128)(2,1)} %wout.1, bf16[1024,512]{1,0:T(8,128)(2,1)} %bitcast.13), custom_call_target="tpu_custom_call" | custom-call | tf_op jit(solution)/shard_map/pallas_call | solution.py:385
  122.2 0.0 copy-start
  122.2 2.3 %copy.10 = bf16[1,2,512,512]{3,2,1,0:T(8,128)(2,1)} copy(bf16[1,2,512,512]{3,2,1,0:T(8,128)(2,1)} %bitcast.14) | data formatting | bytes 2097152
  124.5 0.0 copy-done
  124.5 0.8 copy.11
  (2 shorter events, 0.0 us)
Async XLA Ops:
  0.6 0.7 copy-start.1
  122.2 2.3 %copy-start = (f32[256,512]{1,0:T(8,128)S(1)}, f32[256,512]{1,0:T(8,128)}, u32[]{:S(2)}) copy-start(f32[256,512]{1,0:T(8,128)} %get-tuple-element.9) | copy-start | bytes 1572868

commit v2 on v1

--- a/solution.py
+++ b/solution.py
@@ -32,9 +32,9 @@
     seg, lat, rates, wqkv, wout, cot,
     out, grad,
     xbuf, wbuf, obuf, cotv, ldr, cumr, cumb, kv, intra, states, gains, mine, totals,
-    sbuf, tbuf, attn, gsend, grecv, gdp, gdr,
+    sbuf, tbuf, attn, gsend, gpair, gz, grecv, gdp, gdr, gfin,
     loc, xs, xr, xfs, xfr, ws, wr, wfs, wfr, lds, ldrs, ss, sr, ts, tr, ats, atr,
-    gs, gr, ds_, dr,
+    gps, gpr, gs, gr, ds_, dr,
 ):
     z = lax.axis_index("seq")
     h = lax.axis_index("head")
@@ -52,14 +52,14 @@
     scale = 128 ** (-0.5)
     quarter = (d % 2) * 2 + g
     pair = d + 1 - 2 * (d % 2)
-    partners = ({"dp": pair}, {"groups": 1 - g}, {"dp": pair, "groups": 1 - g})
+    partners = ({"dp": pair}, {"groups": 1 - g})
 
     barrier = pltpu.get_barrier_semaphore()
     count = 0
     for device in (
         [{"seq": lax.rem(z + o, n)} for o in range(1, n)]
-        + [{"head": 1 - h}, {"groups": 1 - g}, {"dp": pair, "groups": 1 - g}]
-        + [{"dp": lax.rem(d + o, dpn)} for o in range(1, dpn)]
+        + [{"head": 1 - h}, {"groups": 1 - g}, {"dp": pair}]
+        + [{"dp": lax.rem(d + 2 * o, dpn)} for o in range(1, dpn // 2)]
     ):
         pl.semaphore_signal(
             barrier, inc=1, device_id=device, device_id_type=pl.DeviceIdType.MESH
@@ -85,7 +85,7 @@
     def lat_block(dst):
         return lat.at[pl.ds(dst * rows, rows)]
 
-    sent = []
+    sent, guarded = [], []
     for o in range(1, n):
         c = remote(rates.at[to(o)], ldr.at[z], lds.at[o - 1], ldrs.at[o - 1], {"seq": to(o)})
         c.start()
@@ -97,10 +97,11 @@
         pltpu.make_async_copy(wout, obuf.at[pl.ds(mult(z * shard, shard), shard), :], loc.at[3]),
         pltpu.make_async_copy(cot, cotv, loc.at[4]),
     ]
-    for o in range(1, n):
-        c = remote(lat_block(to(o)), xslot(z), xs.at[o - 1], xr.at[o - 1], {"seq": to(o)})
-        c.start()
-        sent.append(c)
+    def send_latents():
+        for o in range(1, n):
+            c = remote(lat_block(to(o)), xslot(z), xs.at[o - 1], xr.at[o - 1], {"seq": to(o)})
+            c.start()
+            sent.append(c)
 
     def wsrc(a, row):
         rng = pl.ds(mult(row, piece), piece)
@@ -110,14 +111,88 @@
         rng = pl.ds(mult(row, piece), piece)
         return (wbuf.at[pl.ds(1, 2), rng, :], wbuf.at[0, rng, :], obuf.at[rng, :])[a]
 
-    for a in range(3):
-        for o in range(1, n):
-            c = remote(
-                wsrc(a, quarter * piece), wdst(a, z * shard + quarter * piece),
-                ws.at[a, o - 1], wr.at[a, o - 1], {"seq": to(o)},
-            )
-            c.start()
-            sent.append(c)
+    own_part = quarter * piece
+
+    def wslot(a, src, q):
+        return wdst(a, src * shard + q * piece)
+
+    def when(cond, make):
+        @pl.when(cond)
+        def _():
+            make().start()
+
+        guarded.append((cond, make))
+
+    def launch(a):
+        for way, cond, dev in ((0, z + 1 < n, z + 1), (1, z > 0, z - 1)):
+            when(cond, partial(
+                lambda way, dev: remote(
+                    wsrc(a, own_part), wslot(a, z, quarter), ws.at[a, way, 0], wr.at[a, way, 0], {"seq": dev}
+                ), way, dev))
+
+    def each(fn):
+        for s in range(1, n):
+            for way in range(2):
+                src = z - s if way == 0 else z + s
+                has = src >= 0 if way == 0 else src < n
+                fn(s, way, src, has)
+
+    def chain(a):
+        def visit(s, way, src, has):
+            onward = z + 1 if way == 0 else z - 1
+            more = has & (onward < n if way == 0 else onward >= 0)
+
+            @pl.when(has)
+            def _():
+                slot = wslot(a, src, quarter)
+                remote(slot, slot, ws.at[a, way, s - 1], wr.at[a, way, s - 1], {"seq": z}).wait_recv()
+
+            if s < n - 1:
+                when(more, lambda: remote(
+                    wslot(a, src, quarter), wslot(a, src, quarter),
+                    ws.at[a, way, s], wr.at[a, way, s], {"seq": onward}))
+            for p in range(2):
+                when(has, partial(lambda p: remote(
+                    wslot(a, src, quarter), wslot(a, src, quarter),
+                    wfs.at[a, way, s - 1, p], wfr.at[a, way, s - 1, p], partners[p]), p))
+
+        each(visit)
+
+    def cut(ref, p):
+        lanes = pl.ds(p * (half // 2), half // 2)
+        return ref.at[:, :, lanes] if len(ref.shape) == 3 else ref.at[:, lanes]
+
+    def diagonal(a):
+        def visit(s, way, src, has):
+            for p in range(2):
+                @pl.when(has)
+                def _():
+                    slot = wslot(a, src, other_quarter[p])
+                    remote(slot, slot, wfs.at[a, way, s - 1, p], wfr.at[a, way, s - 1, p], partners[p]).wait_recv()
+
+                when(has, partial(lambda p: remote(
+                    cut(wslot(a, src, other_quarter[p]), p), cut(wslot(a, src, other_quarter[p]), p),
+                    wfs.at[a, way, s - 1, 2 + p], wfr.at[a, way, s - 1, 2 + p], partners[1 - p]), p))
+
+        each(visit)
+
+    def settle(a):
+        def visit(s, way, src, has):
+            @pl.when(has)
+            def _():
+                for p in range(2):
+                    slot = cut(wslot(a, src, other_quarter[2]), p)
+                    remote(slot, slot, wfs.at[a, way, s - 1, 2 + p], wfr.at[a, way, s - 1, 2 + p], partners[1 - p]).wait_recv()
+
+        each(visit)
+
+    other_quarter = (
+        (1 - d % 2) * 2 + g, (d % 2) * 2 + 1 - g, (1 - d % 2) * 2 + 1 - g
+    )
+    launch(0)
+    send_latents()
+    launch(1)
+    launch(2)
     own = remote(lat_block(z), xslot(z), xfs.at[0], xfr.at[0], {"head": 1 - h})
     own.start()
     sent.append(own)
@@ -141,39 +216,25 @@
         for i in range(rows * heads):
             cumb[i, j * chunk:(j + 1) * chunk, :] = jnp.broadcast_to(cumc[:, i:i + 1], (chunk, 128))
 
-    for o in range(1, n):
-        remote(lat_block(z), xslot(frm(o)), xs.at[o - 1], xr.at[o - 1], {"seq": frm(o)}).wait_recv()
-        c = remote(xslot(frm(o)), xslot(frm(o)), xfs.at[o], xfr.at[o], {"head": 1 - h})
-        c.start()
-        sent.append(c)
-
-    def forward(a):
+    def forward_latents():
         for o in range(1, n):
-            slot = wdst(a, frm(o) * shard + quarter * piece)
-            remote(wsrc(a, quarter * piece), slot, ws.at[a, o - 1], wr.at[a, o - 1], {"seq": frm(o)}).wait_recv()
-            for p in range(3):
-                c = remote(slot, slot, wfs.at[a, o - 1, p], wfr.at[a, o - 1, p], partners[p])
-                c.start()
-                sent.append(c)
-
-    other_quarter = (
-        (1 - d % 2) * 2 + g, (d % 2) * 2 + 1 - g, (1 - d % 2) * 2 + 1 - g
-    )
-
-    def forwarded(a):
-        for o in range(1, n):
-            for p in range(3):
-                slot = wdst(a, frm(o) * shard + other_quarter[p] * piece)
-                remote(slot, slot, wfs.at[a, o - 1, p], wfr.at[a, o - 1, p], partners[p]).wait_recv()
-
-    forward(0)
-    forward(1)
+            remote(lat_block(z), xslot(frm(o)), xs.at[o - 1], xr.at[o - 1], {"seq": frm(o)}).wait_recv()
+            c = remote(xslot(frm(o)), xslot(frm(o)), xfs.at[o], xfr.at[o], {"head": 1 - h})
+            c.start()
+            sent.append(c)
+
+    chain(0)
+    chain(1)
+    diagonal(0)
+    forward_latents()
+    diagonal(1)
+    chain(2)
+    settle(0)
     local[1].wait()
     local[2].wait()
     for o in range(n):
         src = z if o == 0 else frm(o)
         remote(xslot_other(src), xslot_other(src), xfs.at[o], xfr.at[o], {"head": 1 - h}).wait_recv()
-    forwarded(0)
 
     def project(c):
         def step(i, carry):
@@ -238,8 +299,8 @@
             remote(mine, sbuf.at[o - 1], ss.at[o - 1], sr.at[o - 1], {"seq": z + o}).start()
             remote(totals, tbuf.at[o - 1], ts.at[o - 1], tr.at[o - 1], {"seq": z + o}).start()
 
-    forward(2)
-    forwarded(1)
+    settle(1)
+    diagonal(2)
     project(0)
 
     def within(idx, carry):
@@ -313,26 +374,35 @@
         def step(i, carry):
             lanes = pl.ds(mult(i * 128, 128), 128)
             part = dot(attn[which, :, lanes], cotv[...], 0, 0) * factor
-            gsend[pl.ds(mult(which * half + i * 128, 128), 128), :] = part.astype(BF)
+            rows_of = min(128, part_rows)
+            per = shard // rows_of
+            for k in range(128 // rows_of):
+                at = (which * half + i * 128) // rows_of + k
+                gsend[at // per, at % per, :, :] = part[k * rows_of:(k + 1) * rows_of].astype(BF)
             return carry
 
         lax.fori_loop(0, heads, step, 0)
 
+    part_rows = shard // 2
+    parity = d % 2
+    group = n // 2
+
+    def give(which):
+        at = pl.ds(mult(which * group, group), group)
+        return remote(
+            gsend.at[at, 1 - parity], gpair.at[at], gps.at[which], gpr.at[which], {"dp": pair}
+        )
+
     grad_half(h)
+    give(h).start()
     for hh in range(heads):
         lanes = pl.ds(hh * 128, 128)
         remote(attn.at[1 - h, :, lanes], attn.at[1 - h, :, lanes], ats.at[hh], atr.at[hh], {"head": 1 - h}).wait_recv()
     grad_half(1 - h)
-    for o in range(1, n):
-        c = remote(
-            gsend.at[pl.ds(mult(to(o) * shard, shard), shard), :], grecv.at[o - 1],
-            gs.at[o - 1], gr.at[o - 1], {"seq": to(o)},
-        )
-        c.start()
-        sent.append(c)
+    give(1 - h).start()
 
     local[3].wait()
-    forwarded(2)
+    settle(2)
 
     def out_step(i, carry):
         toks = pl.ds(mult(i * chunk, chunk), chunk)
@@ -342,24 +412,44 @@
 
     lax.fori_loop(0, chunks, out_step, 0)
 
-    total = gsend[pl.ds(mult(z * shard, shard), shard), :].astype(F32)
+    give(h).wait_recv()
+    give(1 - h).wait_recv()
+    gz[...] = (gsend[:, parity].astype(F32) + gpair[...].astype(F32)).astype(BF)
     for o in range(1, n):
-        remote(gsend.at[pl.ds(0, shard), :], grecv.at[o - 1], gs.at[o - 1], gr.at[o - 1], {"seq": frm(o)}).wait_recv()
-        total = total + grecv[o - 1].astype(F32)
-    gdp[...] = total.astype(BF)
-    gdr[d] = gdp[...]
-    for o in range(1, dpn):
-        peer = lax.rem(d + o, dpn)
-        c = remote(gdp, gdr.at[d], ds_.at[o - 1], dr.at[o - 1], {"dp": peer})
+        c = remote(gz.at[to(o)], grecv.at[o - 1], gs.at[o - 1], gr.at[o - 1], {"seq": to(o)})
         c.start()
         sent.append(c)
-    for o in range(1, dpn):
-        peer = lax.rem(d + dpn - o, dpn)
-        remote(gdp, gdr.at[peer], ds_.at[o - 1], dr.at[o - 1], {"dp": peer}).wait_recv()
-    total = gdr[0].astype(F32)
-    for i in range(1, dpn):
-        total = total + gdr[i].astype(F32)
-    grad[...] = total
+    total = gz[z].astype(F32)
+    for o in range(1, n):
+        remote(gz.at[z], grecv.at[o - 1], gs.at[o - 1], gr.at[o - 1], {"seq": frm(o)}).wait_recv()
+        total = total + grecv[o - 1].astype(F32)
+    if dpn > 2:
+        gdp[...] = total.astype(BF)
+        gdr[d // 2] = gdp[...]
+        for o in range(1, dpn // 2):
+            c = remote(gdp, gdr.at[d // 2], ds_.at[o], dr.at[o], {"dp": lax.rem(d + 2 * o, dpn)})
+            c.start()
+            sent.append(c)
+        for o in range(1, dpn // 2):
+            peer = lax.rem(d + dpn - 2 * o, dpn)
+            remote(gdp, gdr.at[peer // 2], ds_.at[o], dr.at[o], {"dp": peer}).wait_recv()
+        total = gdr[0].astype(F32)
+        for i in range(1, dpn // 2):
+            total = total + gdr[i].astype(F32)
+    gfin[parity] = total.astype(BF)
+    c = remote(gfin.at[parity], gfin.at[parity], ds_.at[0], dr.at[0], {"dp": pair})
+    c.start()
+    remote(gfin.at[1 - parity], gfin.at[1 - parity], ds_.at[0], dr.at[0], {"dp": pair}).wait_recv()
+    for i in range(2):
+        grad[pl.ds(i * part_rows, part_rows), :] = gfin[i].astype(F32)
+    c.wait_send()
+    give(h).wait_send()
+    give(1 - h).wait_send()
+    for cond, make in guarded:
+        @pl.when(cond)
+        def _():
+            make().wait_send()
+
     for c in sent:
         c.wait_send()
 
@@ -407,18 +497,21 @@
             pltpu.VMEM((m, half, 128), BF),
             pltpu.VMEM((m, heads * 8, 128), F32),
             pltpu.VMEM((2, tokens, half), BF),
-            pltpu.VMEM((2 * half, half), BF),
-            pltpu.VMEM((m, shard, half), BF),
-            pltpu.VMEM((shard, half), BF),
-            pltpu.VMEM((dpn, shard, half), BF),
+            pltpu.VMEM((n, 2, shard // 2, half), BF),
+            pltpu.VMEM((n, shard // 2, half), BF),
+            pltpu.VMEM((n, shard // 2, half), BF),
+            pltpu.VMEM((m, shard // 2, half), BF),
+            pltpu.VMEM((shard // 2, half), BF),
+            pltpu.VMEM((dpn // 2, shard // 2, half), BF),
+            pltpu.VMEM((2, shard // 2, half), BF),
             dma((5,)),
             dma((m,)), dma((m,)), dma((n,)), dma((n,)),
-            dma((3, m)), dma((3, m)), dma((3, m, 3)), dma((3, m, 3)),
+            dma((3, 2, m)), dma((3, 2, m)), dma((3, 2, m, 4)), dma((3, 2, m, 4)),
             dma((m,)), dma((m,)),
             dma((m,)), dma((m,)), dma((m,)), dma((m,)),
             dma((heads,)), dma((heads,)),
-            dma((m,)), dma((m,)),
-            dma((dpn - 1,)), dma((dpn - 1,)),
+            dma((2,)), dma((2,)), dma((m,)), dma((m,)),
+            dma((dpn // 2,)), dma((dpn // 2,)),
         ],
         compiler_params=pltpu.CompilerParams(
             collective_id=0, has_side_effects=True, vmem_limit_bytes=56 * 1024 * 1024

time: 126 us -> 110 us (0.87)
  Pallas kernels: 120 us -> 103 us
    pallas_call x1, Pallas kernels: 120 us -> 103 us  [local(): pl.pallas_call(partial(kernel, n, dpn, chunk), out_shape=(jax.ShapeDtypeS...]
where the time goes in v2:
time: 110 us; the launch traced here: 109 us
  Pallas kernels  103 us (94%)
  local copies, waits for them, and re-layouts  3.79 us (3%)
    pallas_call x1, Pallas kernels, local(): pl.pallas_call(partial(kernel, n, dpn, chunk), out_shape=(jax.ShapeDtypeS...  103 us
    unnamed x6, local copies, waits for them, and re-layouts  3.79 us

profile of v2, /device:TPU:8, one launch (start us, length us, event | category | flops | bytes accessed | tf_op | source)
XLA Modules:
  0.0 108.5 jit_solution(13865048154250674654)
XLA Ops:
  0.6 0.0 copy-start.1
  0.7 0.7 copy-done.1
  1.3 0.6 bitcast_select_fusion.rates
  2.0 103.4 %shard_map.77 = (bf16[1024,512]{1,0:T(8,128)(2,1)}, f32[256,512]{1,0:T(8,128)}) custom-call(s32[1,4]{1,0:T(1,128)} %seg.1, bf16[8,128,512]{2,1,0:T(8,128)(2,1)} %bitcast.12, f32[4,8,512]{2,1,0:T(8,128)} %bitcast_select_fusion.rates, bf16[3,256,512]{2,1,0:T(8,128)(2,1)} %bitcast.15, bf16[256,512]{1,0:T(8,128)(2,1)} %wout.1, bf16[1024,512]{1,0:T(8,128)(2,1)} %bitcast.13), custom_call_target="tpu_custom_call" | custom-call | tf_op jit(solution)/shard_map/pallas_call | solution.py:475
  105.4 0.0 copy-start
  105.4 2.3 %copy.10 = bf16[1,2,512,512]{3,2,1,0:T(8,128)(2,1)} copy(bf16[1,2,512,512]{3,2,1,0:T(8,128)(2,1)} %bitcast.14) | data formatting | bytes 2097152
  107.7 0.0 copy-done
  107.7 0.8 copy.11
  (2 shorter events, 0.0 us)
Async XLA Ops:
  0.6 0.7 copy-start.1
  105.4 2.3 %copy-start = (f32[256,512]{1,0:T(8,128)S(1)}, f32[256,512]{1,0:T(8,128)}, u32[]{:S(2)}) copy-start(f32[256,512]{1,0:T(8,128)} %get-tuple-element.9) | copy-start | bytes 1572868

commit v3 on v2

--- a/solution.py
+++ b/solution.py
@@ -190,15 +190,29 @@
         (1 - d % 2) * 2 + g, (d % 2) * 2 + 1 - g, (1 - d % 2) * 2 + 1 - g
     )
     launch(0)
-    send_latents()
     launch(1)
-    launch(2)
     own = remote(lat_block(z), xslot(z), xfs.at[0], xfr.at[0], {"head": 1 - h})
     own.start()
     sent.append(own)
     for c in local:
         c.start()
 
+    def forward_latents():
+        for o in range(1, n):
+            remote(lat_block(z), xslot(frm(o)), xs.at[o - 1], xr.at[o - 1], {"seq": frm(o)}).wait_recv()
+            c = remote(xslot(frm(o)), xslot(frm(o)), xfs.at[o], xfr.at[o], {"head": 1 - h})
+            c.start()
+            sent.append(c)
+
+    chain(0)
+    chain(1)
+    send_latents()
+    launch(2)
+    diagonal(0)
+    diagonal(1)
+    forward_latents()
+    chain(2)
+    settle(0)
     local[0].wait()
     for o in range(1, n):
         remote(rates.at[z], ldr.at[frm(o)], lds.at[o - 1], ldrs.at[o - 1], {"seq": frm(o)}).wait_recv()
@@ -216,20 +230,6 @@
         for i in range(rows * heads):
             cumb[i, j * chunk:(j + 1) * chunk, :] = jnp.broadcast_to(cumc[:, i:i + 1], (chunk, 128))
 
-    def forward_latents():
-        for o in range(1, n):
-            remote(lat_block(z), xslot(frm(o)), xs.at[o - 1], xr.at[o - 1], {"seq": frm(o)}).wait_recv()
-            c = remote(xslot(frm(o)), xslot(frm(o)), xfs.at[o], xfr.at[o], {"head": 1 - h})
-            c.start()
-            sent.append(c)
-
-    chain(0)
-    chain(1)
-    diagonal(0)
-    forward_latents()
-    diagonal(1)
-    chain(2)
-    settle(0)
     local[1].wait()
     local[2].wait()
     for o in range(n):
@@ -401,6 +401,18 @@
     grad_half(1 - h)
     give(1 - h).start()
 
+    def pass_on(which):
+        give(which).wait_recv()
+        at = pl.ds(mult(which * group, group), group)
+        gz[at] = (gsend[at, parity].astype(F32) + gpair[at].astype(F32)).astype(BF)
+        for k in range(group):
+            block = which * group + k
+            o = lax.rem(block - z + n, n)
+            slot = jnp.maximum(o - 1, 0)
+            when(o > 0, partial(lambda block, slot: remote(
+                gz.at[block], grecv.at[slot], gs.at[slot], gr.at[slot], {"seq": block}), block, slot))
+
+    pass_on(h)
     local[3].wait()
     settle(2)
 
@@ -412,13 +424,7 @@
 
     lax.fori_loop(0, chunks, out_step, 0)
 
-    give(h).wait_recv()
-    give(1 - h).wait_recv()
-    gz[...] = (gsend[:, parity].astype(F32) + gpair[...].astype(F32)).astype(BF)
-    for o in range(1, n):
-        c = remote(gz.at[to(o)], grecv.at[o - 1], gs.at[o - 1], gr.at[o - 1], {"seq": to(o)})
-        c.start()
-        sent.append(c)
+    pass_on(1 - h)
     total = gz[z].astype(F32)
     for o in range(1, n):
         remote(gz.at[z], grecv.at[o - 1], gs.at[o - 1], gr.at[o - 1], {"seq": frm(o)}).wait_recv()

time: 110 us -> 101 us (0.918); the launches traced: 109 us -> 101 us
  Pallas kernels: 103 us -> 95.5 us
    pallas_call x1, Pallas kernels: 103 us -> 95.5 us  [local(): pl.pallas_call(partial(kernel, n, dpn, chunk), out_shape=(jax.ShapeDtypeS...]
where the time goes in v3:
time: 101 us
  Pallas kernels  95.5 us (95%)
  local copies, waits for them, and re-layouts  3.79 us (4%)
    pallas_call x1, Pallas kernels, local(): pl.pallas_call(partial(kernel, n, dpn, chunk), out_shape=(jax.ShapeDtypeS...  95.5 us
    unnamed x6, local copies, waits for them, and re-layouts  3.79 us

profile of v3, /device:TPU:8, one launch (start us, length us, event | category | flops | bytes accessed | tf_op | source)
XLA Modules:
  0.0 100.7 jit_solution(15014715526918034518)
XLA Ops:
  0.6 0.0 copy-start.1
  0.7 0.7 copy-done.1
  1.3 0.6 bitcast_select_fusion.rates
  2.0 95.5 %shard_map.77 = (bf16[1024,512]{1,0:T(8,128)(2,1)}, f32[256,512]{1,0:T(8,128)}) custom-call(s32[1,4]{1,0:T(1,128)} %seg.1, bf16[8,128,512]{2,1,0:T(8,128)(2,1)} %bitcast.12, f32[4,8,512]{2,1,0:T(8,128)} %bitcast_select_fusion.rates, bf16[3,256,512]{2,1,0:T(8,128)(2,1)} %bitcast.15, bf16[256,512]{1,0:T(8,128)(2,1)} %wout.1, bf16[1024,512]{1,0:T(8,128)(2,1)} %bitcast.13), custom_call_target="tpu_custom_call" | custom-call | tf_op jit(solution)/shard_map/pallas_call | solution.py:481
  97.5 0.0 copy-start
  97.5 2.3 %copy.10 = bf16[1,2,512,512]{3,2,1,0:T(8,128)(2,1)} copy(bf16[1,2,512,512]{3,2,1,0:T(8,128)(2,1)} %bitcast.14) | data formatting | bytes 2097152
  99.9 0.0 copy-done
  99.9 0.8 copy.11
  (2 shorter events, 0.0 us)
Async XLA Ops:
  0.6 0.7 copy-start.1
  97.5 2.3 %copy-start = (f32[256,512]{1,0:T(8,128)S(1)}, f32[256,512]{1,0:T(8,128)}, u32[]{:S(2)}) copy-start(f32[256,512]{1,0:T(8,128)} %get-tuple-element.9) | copy-start | bytes 1572868
